TPU v7x, 512 devices: a whole 4x8x8 slice. The times are simulated.
512 devices in a mesh: loop: 32 (over y_hi, x, core), grp: 16 (over y_lo, z).
Axes of the slice: x: 4, y: 8 (y_hi: 4, y_lo: 2; y = y_hi * 2 + y_lo), z: 8, core: 2. Of those that a mesh axis runs over, the one named last changes fastest.
Arguments:
- image_emb: bfloat16 [8192, 1152], P(('loop', 'grp')), may hold values from -6 to 6
- text_emb: bfloat16 [8192, 1152], P(('loop', 'grp')), may hold values from -6 to 6
- log_scale: float32 [1], replicated, may hold values from 4.2 to 4.8
- bias: float32 [1], replicated, may hold values from -4 to -2
Outputs:
- image_grad: float32 [8192, 1152], P(('loop', 'grp'))
- text_grad: float32 [8192, 1152], P(('loop', 'grp'))
All inputs are finite; a program needn't handle non-finite values.
Results may differ from a plain program's by a relative error of at most 0.008.
Values may be sent and summed in bfloat16 or wider, within the bound.
A program may use at most 64 MiB of HBM per device.

v0:
```python
import jax
import jax.numpy as jnp
from jax import lax
from jax.sharding import PartitionSpec as P

EPS = 1e-06


def from_behind(value, axis, steps):
    count = lax.axis_size(axis)
    pairs = [(source, (source + steps) % count) for source in range(count)]
    return lax.ppermute(value, axis, pairs)


def normalize(values):
    wide = values.astype(jnp.float32)
    length = jnp.sqrt(jnp.sum(wide * wide, axis=-1, keepdims=True) + EPS)
    return (wide / length, length)


def norm_back(unit_rows, length, upstream):
    along = jnp.sum(unit_rows * upstream, axis=-1, keepdims=True)
    return (upstream - unit_rows * along) / length


def move_text(text_rows):
    return from_behind(text_rows, "loop", 1)


def move_grads(text_grad):
    return from_behind(text_grad, "loop", 1)


def per_device(image_emb, text_emb, log_scale, bias):
    row_count, feat_width = image_emb.shape
    loop_count = lax.axis_size("loop")
    groups = lax.axis_size("grp")
    loop_at = lax.axis_index("loop")
    group_at = lax.axis_index("grp")
    logit_scale = jnp.exp(log_scale[0])
    offset = bias[0]
    img_unit, img_length = normalize(image_emb)
    txt_unit, txt_length = normalize(text_emb)
    image_block = lax.all_gather(img_unit.astype(jnp.bfloat16), "grp", axis=0, tiled=True)
    block_rows = groups * row_count
    image_ids = loop_at * block_rows + jnp.arange(block_rows, dtype=jnp.int32)
    text_rows = txt_unit.astype(jnp.bfloat16)

    def text_ids(turn_index):
        source = (loop_at - turn_index) % loop_count
        return (source * groups + group_at) * row_count + jnp.arange(row_count, dtype=jnp.int32)

    def station(turn_index, moving, summed, grads_seen, texts_seen):
        logits = (
            logit_scale
            * jnp.einsum("id,kd->ik", image_block, moving, preferred_element_type=jnp.float32)
            + offset
        )
        labels = (image_ids[:, None] == text_ids(turn_index)[None, :]).astype(jnp.float32)
        grad_low = (logit_scale * (jax.nn.sigmoid(logits) - labels)).astype(jnp.bfloat16)
        summed = summed + jnp.einsum(
            "ik,id->kd", grad_low, image_block, preferred_element_type=jnp.float32
        )
        grads_seen = lax.dynamic_update_slice(grads_seen, grad_low, (0, turn_index * row_count))
        texts_seen = lax.dynamic_update_slice(texts_seen, moving, (turn_index * row_count, 0))
        return (summed, grads_seen, texts_seen)

    text_grad = jnp.zeros((row_count, feat_width), jnp.float32)
    grad_table = jnp.zeros((block_rows, loop_count * row_count), jnp.bfloat16)
    text_table = jnp.zeros((loop_count * row_count, feat_width), jnp.bfloat16)
    text_grad, grad_table, text_table = station(
        jnp.int32(0), text_rows, text_grad, grad_table, text_table
    )

    def turn(turn_index, loop_state):
        moving, summed, grads_seen, texts_seen = loop_state
        moving = move_text(moving)
        summed = move_grads(summed)
        summed, grads_seen, texts_seen = station(turn_index, moving, summed, grads_seen, texts_seen)
        return (moving, summed, grads_seen, texts_seen)

    text_rows, text_grad, grad_table, text_table = lax.fori_loop(
        1, loop_count, turn, (text_rows, text_grad, grad_table, text_table)
    )
    text_grad = move_grads(text_grad)
    image_terms = jnp.dot(grad_table, text_table, preferred_element_type=jnp.float32)
    image_sum = lax.psum_scatter(image_terms, "grp", scatter_dimension=0, tiled=True)
    return (norm_back(img_unit, img_length, image_sum), norm_back(txt_unit, txt_length, text_grad))


def solution(mesh):
    return jax.shard_map(
        per_device,
        mesh=mesh,
        in_specs=(P(("loop", "grp"), None), P(("loop", "grp"), None), P(), P()),
        out_specs=(P(("loop", "grp"), None), P(("loop", "grp"), None)),
        check_vma=False,
    )
```

profile of v0, /device:TPU:4, one launch (start us, length us, event | category | flops | bytes accessed | tf_op | source)
XLA Modules:
  0.0 511.3 jit_solution(7196596203872255199)
XLA Ops:
  12.1 42.7 %all_gather.3 = bf16[256,1152]{1,0:T(8,128)(2,1)S(1)} all-gather(bf16[16,1152]{1,0:T(8,128)(2,1)S(1)} %fusion.21), channel_id=1, replica_groups=mesh['loop'=32,'grp'=16] {'grp'}, dimensions={0}, use_global_device_ids=true | all-gather | bytes 626688 | tf_op jit(solution)/shard_map/all_gather | solution.py:44
  55.4 350.3 %while.22 = (s32[]{:T(128)}, bf16[16,1152]{1,0:T(8,128)(2,1)S(1)}, f32[16,1152]{1,0:T(8,128)S(1)}, bf16[256,512]{0,1:T(8,128)(2,1)S(1)}, bf16[512,1152]{1,0:T(8,...) while((s32[]{:T(128)}, bf16[16,1152]{1,0:T(8,128)(2,1)S(1)}, ...), condition=%wide.region_3.4_spmd.clone, body=%wide.region_2.3_spmd.clone.sunk | while | flops 18934052 | bytes 1981456 | solution.py:82
  73.0 6.9 %collective-permute-start.1 = (f32[16,1152]{1,0:T(8,128)S(1)}, f32[16,1152]{1,0:T(8,128)S(1)}, u32[]{:S(2)}, u32[]{:S(2)}) collective-permute-start(f32[16,1152]{1,0:T(8,128)S(1)} %get-tuple-element.411), channel_id=1, source_target_pairs={{0,16},{16,32},{32,48},{48,64},{64,80},{80,96},{96,112},{112,128},... | collective-permute-start | bytes 221192 | tf_op jit(solution)/shard_map/while/body/eval_jaxpr/ppermute | solution.py:12
  83.7 7.8 %collective-permute-start.1 = (f32[16,1152]{1,0:T(8,128)S(1)}, f32[16,1152]{1,0:T(8,128)S(1)}, u32[]{:S(2)}, u32[]{:S(2)}) collective-permute-start(f32[16,1152]{1,0:T(8,128)S(1)} %get-tuple-element.411), channel_id=1, source_target_pairs={{0,16},{16,32},{32,48},{48,64},{64,80},{80,96},{96,112},{112,128},... | collective-permute-start | bytes 221192 | tf_op jit(solution)/shard_map/while/body/eval_jaxpr/ppermute | solution.py:12
  95.3 7.0 %collective-permute-start.1 = (f32[16,1152]{1,0:T(8,128)S(1)}, f32[16,1152]{1,0:T(8,128)S(1)}, u32[]{:S(2)}, u32[]{:S(2)}) collective-permute-start(f32[16,1152]{1,0:T(8,128)S(1)} %get-tuple-element.411), channel_id=1, source_target_pairs={{0,16},{16,32},{32,48},{48,64},{64,80},{80,96},{96,112},{112,128},... | collective-permute-start | bytes 221192 | tf_op jit(solution)/shard_map/while/body/eval_jaxpr/ppermute | solution.py:12
  106.4 7.1 %collective-permute-start.1 = (f32[16,1152]{1,0:T(8,128)S(1)}, f32[16,1152]{1,0:T(8,128)S(1)}, u32[]{:S(2)}, u32[]{:S(2)}) collective-permute-start(f32[16,1152]{1,0:T(8,128)S(1)} %get-tuple-element.411), channel_id=1, source_target_pairs={{0,16},{16,32},{32,48},{48,64},{64,80},{80,96},{96,112},{112,128},... | collective-permute-start | bytes 221192 | tf_op jit(solution)/shard_map/while/body/eval_jaxpr/ppermute | solution.py:12
  117.4 7.0 %collective-permute-start.1 = (f32[16,1152]{1,0:T(8,128)S(1)}, f32[16,1152]{1,0:T(8,128)S(1)}, u32[]{:S(2)}, u32[]{:S(2)}) collective-permute-start(f32[16,1152]{1,0:T(8,128)S(1)} %get-tuple-element.411), channel_id=1, source_target_pairs={{0,16},{16,32},{32,48},{48,64},{64,80},{80,96},{96,112},{112,128},... | collective-permute-start | bytes 221192 | tf_op jit(solution)/shard_map/while/body/eval_jaxpr/ppermute | solution.py:12
  128.2 7.0 %collective-permute-start.1 = (f32[16,1152]{1,0:T(8,128)S(1)}, f32[16,1152]{1,0:T(8,128)S(1)}, u32[]{:S(2)}, u32[]{:S(2)}) collective-permute-start(f32[16,1152]{1,0:T(8,128)S(1)} %get-tuple-element.411), channel_id=1, source_target_pairs={{0,16},{16,32},{32,48},{48,64},{64,80},{80,96},{96,112},{112,128},... | collective-permute-start | bytes 221192 | tf_op jit(solution)/shard_map/while/body/eval_jaxpr/ppermute | solution.py:12
  139.0 7.0 %collective-permute-start.1 = (f32[16,1152]{1,0:T(8,128)S(1)}, f32[16,1152]{1,0:T(8,128)S(1)}, u32[]{:S(2)}, u32[]{:S(2)}) collective-permute-start(f32[16,1152]{1,0:T(8,128)S(1)} %get-tuple-element.411), channel_id=1, source_target_pairs={{0,16},{16,32},{32,48},{48,64},{64,80},{80,96},{96,112},{112,128},... | collective-permute-start | bytes 221192 | tf_op jit(solution)/shard_map/while/body/eval_jaxpr/ppermute | solution.py:12
  149.8 7.0 %collective-permute-start.1 = (f32[16,1152]{1,0:T(8,128)S(1)}, f32[16,1152]{1,0:T(8,128)S(1)}, u32[]{:S(2)}, u32[]{:S(2)}) collective-permute-start(f32[16,1152]{1,0:T(8,128)S(1)} %get-tuple-element.411), channel_id=1, source_target_pairs={{0,16},{16,32},{32,48},{48,64},{64,80},{80,96},{96,112},{112,128},... | collective-permute-start | bytes 221192 | tf_op jit(solution)/shard_map/while/body/eval_jaxpr/ppermute | solution.py:12
  160.6 7.0 %collective-permute-start.1 = (f32[16,1152]{1,0:T(8,128)S(1)}, f32[16,1152]{1,0:T(8,128)S(1)}, u32[]{:S(2)}, u32[]{:S(2)}) collective-permute-start(f32[16,1152]{1,0:T(8,128)S(1)} %get-tuple-element.411), channel_id=1, source_target_pairs={{0,16},{16,32},{32,48},{48,64},{64,80},{80,96},{96,112},{112,128},... | collective-permute-start | bytes 221192 | tf_op jit(solution)/shard_map/while/body/eval_jaxpr/ppermute | solution.py:12
  171.5 7.0 %collective-permute-start.1 = (f32[16,1152]{1,0:T(8,128)S(1)}, f32[16,1152]{1,0:T(8,128)S(1)}, u32[]{:S(2)}, u32[]{:S(2)}) collective-permute-start(f32[16,1152]{1,0:T(8,128)S(1)} %get-tuple-element.411), channel_id=1, source_target_pairs={{0,16},{16,32},{32,48},{48,64},{64,80},{80,96},{96,112},{112,128},... | collective-permute-start | bytes 221192 | tf_op jit(solution)/shard_map/while/body/eval_jaxpr/ppermute | solution.py:12
  182.3 7.0 %collective-permute-start.1 = (f32[16,1152]{1,0:T(8,128)S(1)}, f32[16,1152]{1,0:T(8,128)S(1)}, u32[]{:S(2)}, u32[]{:S(2)}) collective-permute-start(f32[16,1152]{1,0:T(8,128)S(1)} %get-tuple-element.411), channel_id=1, source_target_pairs={{0,16},{16,32},{32,48},{48,64},{64,80},{80,96},{96,112},{112,128},... | collective-permute-start | bytes 221192 | tf_op jit(solution)/shard_map/while/body/eval_jaxpr/ppermute | solution.py:12
  193.7 7.1 %collective-permute-start.1 = (f32[16,1152]{1,0:T(8,128)S(1)}, f32[16,1152]{1,0:T(8,128)S(1)}, u32[]{:S(2)}, u32[]{:S(2)}) collective-permute-start(f32[16,1152]{1,0:T(8,128)S(1)} %get-tuple-element.411), channel_id=1, source_target_pairs={{0,16},{16,32},{32,48},{48,64},{64,80},{80,96},{96,112},{112,128},... | collective-permute-start | bytes 221192 | tf_op jit(solution)/shard_map/while/body/eval_jaxpr/ppermute | solution.py:12
  204.6 7.8 %collective-permute-start.1 = (f32[16,1152]{1,0:T(8,128)S(1)}, f32[16,1152]{1,0:T(8,128)S(1)}, u32[]{:S(2)}, u32[]{:S(2)}) collective-permute-start(f32[16,1152]{1,0:T(8,128)S(1)} %get-tuple-element.411), channel_id=1, source_target_pairs={{0,16},{16,32},{32,48},{48,64},{64,80},{80,96},{96,112},{112,128},... | collective-permute-start | bytes 221192 | tf_op jit(solution)/shard_map/while/body/eval_jaxpr/ppermute | solution.py:12
  216.2 7.0 %collective-permute-start.1 = (f32[16,1152]{1,0:T(8,128)S(1)}, f32[16,1152]{1,0:T(8,128)S(1)}, u32[]{:S(2)}, u32[]{:S(2)}) collective-permute-start(f32[16,1152]{1,0:T(8,128)S(1)} %get-tuple-element.411), channel_id=1, source_target_pairs={{0,16},{16,32},{32,48},{48,64},{64,80},{80,96},{96,112},{112,128},... | collective-permute-start | bytes 221192 | tf_op jit(solution)/shard_map/while/body/eval_jaxpr/ppermute | solution.py:12
  227.0 7.0 %collective-permute-start.1 = (f32[16,1152]{1,0:T(8,128)S(1)}, f32[16,1152]{1,0:T(8,128)S(1)}, u32[]{:S(2)}, u32[]{:S(2)}) collective-permute-start(f32[16,1152]{1,0:T(8,128)S(1)} %get-tuple-element.411), channel_id=1, source_target_pairs={{0,16},{16,32},{32,48},{48,64},{64,80},{80,96},{96,112},{112,128},... | collective-permute-start | bytes 221192 | tf_op jit(solution)/shard_map/while/body/eval_jaxpr/ppermute | solution.py:12
  238.6 6.2 %collective-permute-start.1 = (f32[16,1152]{1,0:T(8,128)S(1)}, f32[16,1152]{1,0:T(8,128)S(1)}, u32[]{:S(2)}, u32[]{:S(2)}) collective-permute-start(f32[16,1152]{1,0:T(8,128)S(1)} %get-tuple-element.411), channel_id=1, source_target_pairs={{0,16},{16,32},{32,48},{48,64},{64,80},{80,96},{96,112},{112,128},... | collective-permute-start | bytes 221192 | tf_op jit(solution)/shard_map/while/body/eval_jaxpr/ppermute | solution.py:12
  250.7 5.1 collective-permute-start.1
  278.3 4.0 collective-permute-done
  290.3 4.0 collective-permute-done
  302.4 4.0 collective-permute-done
  314.4 4.3 collective-permute-done
  326.4 4.3 collective-permute-done
  338.4 4.3 collective-permute-done
  350.5 4.3 collective-permute-done
  362.5 4.5 collective-permute-done
  374.5 4.6 collective-permute-done
  386.6 4.6 collective-permute-done
  398.6 4.6 collective-permute-done
  409.2 8.1 %collective-permute-done.2 = f32[16,1152]{1,0:T(8,128)S(1)} collective-permute-done((f32[16,1152]{1,0:T(8,128)S(1)}, f32[16,1152]{1,0:T(8,128)S(1)}, u32[]{:S(2)}, u32[]{:S(2)}) %collective-permute-start.2) | collective-permute-done | bytes 73760 | tf_op jit(solution)/shard_map/ppermute | solution.py:12
  418.3 83.5 %reduce-scatter.2.cloned.1.call-done = f32[16,1152]{1,0:T(8,128)} async-done(((f32[256,1152]{1,0:T(8,128)}), f32[16,1152]{1,0:T(8,128)}) %reduce-scatter.2.cloned.1.call-update) | async-done | bytes 73744 | tf_op jit(solution)/shard_map/reduce_scatter | solution.py:87
  (306 shorter events, 193.1 us)
Async XLA Ops:
  7.2 494.6 %reduce-scatter.2.cloned.1.call-start = ((), (), s32[]{:S(2)}) async-start(), calls=%async_computation.1 | async-start | bytes 1253376 | tf_op jit(solution)/shard_map/reduce_scatter | solution.py:87
  81.2 10.4 %collective-permute-start = (bf16[16,1152]{1,0:T(8,128)(2,1)S(1)}, bf16[16,1152]{1,0:T(8,128)(2,1)S(1)}, u32[]{:S(2)}, u32[]{:S(2)}) collective-permute-start(bf16[16,1152]{1,0:T(8,128)(2,1)S(1)} %get-tuple-element.410), channel_id=1, source_target_pairs={{0,16},{16,32},{32,48},{48,64},{64,80},{80,96},{96,112},{112,128},... | collective-permute-start | bytes 110600 | tf_op jit(solution)/shard_map/while/body/eval_jaxpr/ppermute | solution.py:12
  92.8 9.6 %collective-permute-start = (bf16[16,1152]{1,0:T(8,128)(2,1)S(1)}, bf16[16,1152]{1,0:T(8,128)(2,1)S(1)}, u32[]{:S(2)}, u32[]{:S(2)}) collective-permute-start(bf16[16,1152]{1,0:T(8,128)(2,1)S(1)} %get-tuple-element.410), channel_id=1, source_target_pairs={{0,16},{16,32},{32,48},{48,64},{64,80},{80,96},{96,112},{112,128},... | collective-permute-start | bytes 110600 | tf_op jit(solution)/shard_map/while/body/eval_jaxpr/ppermute | solution.py:12
  103.6 10.0 %collective-permute-start = (bf16[16,1152]{1,0:T(8,128)(2,1)S(1)}, bf16[16,1152]{1,0:T(8,128)(2,1)S(1)}, u32[]{:S(2)}, u32[]{:S(2)}) collective-permute-start(bf16[16,1152]{1,0:T(8,128)(2,1)S(1)} %get-tuple-element.410), channel_id=1, source_target_pairs={{0,16},{16,32},{32,48},{48,64},{64,80},{80,96},{96,112},{112,128},... | collective-permute-start | bytes 110600 | tf_op jit(solution)/shard_map/while/body/eval_jaxpr/ppermute | solution.py:12
  114.8 9.6 %collective-permute-start = (bf16[16,1152]{1,0:T(8,128)(2,1)S(1)}, bf16[16,1152]{1,0:T(8,128)(2,1)S(1)}, u32[]{:S(2)}, u32[]{:S(2)}) collective-permute-start(bf16[16,1152]{1,0:T(8,128)(2,1)S(1)} %get-tuple-element.410), channel_id=1, source_target_pairs={{0,16},{16,32},{32,48},{48,64},{64,80},{80,96},{96,112},{112,128},... | collective-permute-start | bytes 110600 | tf_op jit(solution)/shard_map/while/body/eval_jaxpr/ppermute | solution.py:12
  125.6 9.6 %collective-permute-start = (bf16[16,1152]{1,0:T(8,128)(2,1)S(1)}, bf16[16,1152]{1,0:T(8,128)(2,1)S(1)}, u32[]{:S(2)}, u32[]{:S(2)}) collective-permute-start(bf16[16,1152]{1,0:T(8,128)(2,1)S(1)} %get-tuple-element.410), channel_id=1, source_target_pairs={{0,16},{16,32},{32,48},{48,64},{64,80},{80,96},{96,112},{112,128},... | collective-permute-start | bytes 110600 | tf_op jit(solution)/shard_map/while/body/eval_jaxpr/ppermute | solution.py:12
  136.4 9.6 %collective-permute-start = (bf16[16,1152]{1,0:T(8,128)(2,1)S(1)}, bf16[16,1152]{1,0:T(8,128)(2,1)S(1)}, u32[]{:S(2)}, u32[]{:S(2)}) collective-permute-start(bf16[16,1152]{1,0:T(8,128)(2,1)S(1)} %get-tuple-element.410), channel_id=1, source_target_pairs={{0,16},{16,32},{32,48},{48,64},{64,80},{80,96},{96,112},{112,128},... | collective-permute-start | bytes 110600 | tf_op jit(solution)/shard_map/while/body/eval_jaxpr/ppermute | solution.py:12
  147.3 9.6 %collective-permute-start = (bf16[16,1152]{1,0:T(8,128)(2,1)S(1)}, bf16[16,1152]{1,0:T(8,128)(2,1)S(1)}, u32[]{:S(2)}, u32[]{:S(2)}) collective-permute-start(bf16[16,1152]{1,0:T(8,128)(2,1)S(1)} %get-tuple-element.410), channel_id=1, source_target_pairs={{0,16},{16,32},{32,48},{48,64},{64,80},{80,96},{96,112},{112,128},... | collective-permute-start | bytes 110600 | tf_op jit(solution)/shard_map/while/body/eval_jaxpr/ppermute | solution.py:12
  158.1 9.6 %collective-permute-start = (bf16[16,1152]{1,0:T(8,128)(2,1)S(1)}, bf16[16,1152]{1,0:T(8,128)(2,1)S(1)}, u32[]{:S(2)}, u32[]{:S(2)}) collective-permute-start(bf16[16,1152]{1,0:T(8,128)(2,1)S(1)} %get-tuple-element.410), channel_id=1, source_target_pairs={{0,16},{16,32},{32,48},{48,64},{64,80},{80,96},{96,112},{112,128},... | collective-permute-start | bytes 110600 | tf_op jit(solution)/shard_map/while/body/eval_jaxpr/ppermute | solution.py:12
  168.9 9.6 %collective-permute-start = (bf16[16,1152]{1,0:T(8,128)(2,1)S(1)}, bf16[16,1152]{1,0:T(8,128)(2,1)S(1)}, u32[]{:S(2)}, u32[]{:S(2)}) collective-permute-start(bf16[16,1152]{1,0:T(8,128)(2,1)S(1)} %get-tuple-element.410), channel_id=1, source_target_pairs={{0,16},{16,32},{32,48},{48,64},{64,80},{80,96},{96,112},{112,128},... | collective-permute-start | bytes 110600 | tf_op jit(solution)/shard_map/while/body/eval_jaxpr/ppermute | solution.py:12
  179.7 9.6 %collective-permute-start = (bf16[16,1152]{1,0:T(8,128)(2,1)S(1)}, bf16[16,1152]{1,0:T(8,128)(2,1)S(1)}, u32[]{:S(2)}, u32[]{:S(2)}) collective-permute-start(bf16[16,1152]{1,0:T(8,128)(2,1)S(1)} %get-tuple-element.410), channel_id=1, source_target_pairs={{0,16},{16,32},{32,48},{48,64},{64,80},{80,96},{96,112},{112,128},... | collective-permute-start | bytes 110600 | tf_op jit(solution)/shard_map/while/body/eval_jaxpr/ppermute | solution.py:12
  190.5 10.3 %collective-permute-start = (bf16[16,1152]{1,0:T(8,128)(2,1)S(1)}, bf16[16,1152]{1,0:T(8,128)(2,1)S(1)}, u32[]{:S(2)}, u32[]{:S(2)}) collective-permute-start(bf16[16,1152]{1,0:T(8,128)(2,1)S(1)} %get-tuple-element.410), channel_id=1, source_target_pairs={{0,16},{16,32},{32,48},{48,64},{64,80},{80,96},{96,112},{112,128},... | collective-permute-start | bytes 110600 | tf_op jit(solution)/shard_map/while/body/eval_jaxpr/ppermute | solution.py:12
  202.0 10.4 %collective-permute-start = (bf16[16,1152]{1,0:T(8,128)(2,1)S(1)}, bf16[16,1152]{1,0:T(8,128)(2,1)S(1)}, u32[]{:S(2)}, u32[]{:S(2)}) collective-permute-start(bf16[16,1152]{1,0:T(8,128)(2,1)S(1)} %get-tuple-element.410), channel_id=1, source_target_pairs={{0,16},{16,32},{32,48},{48,64},{64,80},{80,96},{96,112},{112,128},... | collective-permute-start | bytes 110600 | tf_op jit(solution)/shard_map/while/body/eval_jaxpr/ppermute | solution.py:12
  213.6 9.6 %collective-permute-start = (bf16[16,1152]{1,0:T(8,128)(2,1)S(1)}, bf16[16,1152]{1,0:T(8,128)(2,1)S(1)}, u32[]{:S(2)}, u32[]{:S(2)}) collective-permute-start(bf16[16,1152]{1,0:T(8,128)(2,1)S(1)} %get-tuple-element.410), channel_id=1, source_target_pairs={{0,16},{16,32},{32,48},{48,64},{64,80},{80,96},{96,112},{112,128},... | collective-permute-start | bytes 110600 | tf_op jit(solution)/shard_map/while/body/eval_jaxpr/ppermute | solution.py:12
  238.6 9.9 %collective-permute-start.1 = (f32[16,1152]{1,0:T(8,128)S(1)}, f32[16,1152]{1,0:T(8,128)S(1)}, u32[]{:S(2)}, u32[]{:S(2)}) collective-permute-start(f32[16,1152]{1,0:T(8,128)S(1)} %get-tuple-element.411), channel_id=1, source_target_pairs={{0,16},{16,32},{32,48},{48,64},{64,80},{80,96},{96,112},{112,128},... | collective-permute-start | bytes 221192 | tf_op jit(solution)/shard_map/while/body/eval_jaxpr/ppermute | solution.py:12
  250.7 9.9 %collective-permute-start.1 = (f32[16,1152]{1,0:T(8,128)S(1)}, f32[16,1152]{1,0:T(8,128)S(1)}, u32[]{:S(2)}, u32[]{:S(2)}) collective-permute-start(f32[16,1152]{1,0:T(8,128)S(1)} %get-tuple-element.411), channel_id=1, source_target_pairs={{0,16},{16,32},{32,48},{48,64},{64,80},{80,96},{96,112},{112,128},... | collective-permute-start | bytes 221192 | tf_op jit(solution)/shard_map/while/body/eval_jaxpr/ppermute | solution.py:12
  262.7 9.9 %collective-permute-start.1 = (f32[16,1152]{1,0:T(8,128)S(1)}, f32[16,1152]{1,0:T(8,128)S(1)}, u32[]{:S(2)}, u32[]{:S(2)}) collective-permute-start(f32[16,1152]{1,0:T(8,128)S(1)} %get-tuple-element.411), channel_id=1, source_target_pairs={{0,16},{16,32},{32,48},{48,64},{64,80},{80,96},{96,112},{112,128},... | collective-permute-start | bytes 221192 | tf_op jit(solution)/shard_map/while/body/eval_jaxpr/ppermute | solution.py:12
  274.7 9.9 %collective-permute-start.1 = (f32[16,1152]{1,0:T(8,128)S(1)}, f32[16,1152]{1,0:T(8,128)S(1)}, u32[]{:S(2)}, u32[]{:S(2)}) collective-permute-start(f32[16,1152]{1,0:T(8,128)S(1)} %get-tuple-element.411), channel_id=1, source_target_pairs={{0,16},{16,32},{32,48},{48,64},{64,80},{80,96},{96,112},{112,128},... | collective-permute-start | bytes 221192 | tf_op jit(solution)/shard_map/while/body/eval_jaxpr/ppermute | solution.py:12
  286.8 9.9 %collective-permute-start.1 = (f32[16,1152]{1,0:T(8,128)S(1)}, f32[16,1152]{1,0:T(8,128)S(1)}, u32[]{:S(2)}, u32[]{:S(2)}) collective-permute-start(f32[16,1152]{1,0:T(8,128)S(1)} %get-tuple-element.411), channel_id=1, source_target_pairs={{0,16},{16,32},{32,48},{48,64},{64,80},{80,96},{96,112},{112,128},... | collective-permute-start | bytes 221192 | tf_op jit(solution)/shard_map/while/body/eval_jaxpr/ppermute | solution.py:12
  298.8 9.9 %collective-permute-start.1 = (f32[16,1152]{1,0:T(8,128)S(1)}, f32[16,1152]{1,0:T(8,128)S(1)}, u32[]{:S(2)}, u32[]{:S(2)}) collective-permute-start(f32[16,1152]{1,0:T(8,128)S(1)} %get-tuple-element.411), channel_id=1, source_target_pairs={{0,16},{16,32},{32,48},{48,64},{64,80},{80,96},{96,112},{112,128},... | collective-permute-start | bytes 221192 | tf_op jit(solution)/shard_map/while/body/eval_jaxpr/ppermute | solution.py:12
  308.9 9.8 %collective-permute-start = (bf16[16,1152]{1,0:T(8,128)(2,1)S(1)}, bf16[16,1152]{1,0:T(8,128)(2,1)S(1)}, u32[]{:S(2)}, u32[]{:S(2)}) collective-permute-start(bf16[16,1152]{1,0:T(8,128)(2,1)S(1)} %get-tuple-element.410), channel_id=1, source_target_pairs={{0,16},{16,32},{32,48},{48,64},{64,80},{80,96},{96,112},{112,128},... | collective-permute-start | bytes 110600 | tf_op jit(solution)/shard_map/while/body/eval_jaxpr/ppermute | solution.py:12
  310.8 10.2 %collective-permute-start.1 = (f32[16,1152]{1,0:T(8,128)S(1)}, f32[16,1152]{1,0:T(8,128)S(1)}, u32[]{:S(2)}, u32[]{:S(2)}) collective-permute-start(f32[16,1152]{1,0:T(8,128)S(1)} %get-tuple-element.411), channel_id=1, source_target_pairs={{0,16},{16,32},{32,48},{48,64},{64,80},{80,96},{96,112},{112,128},... | collective-permute-start | bytes 221192 | tf_op jit(solution)/shard_map/while/body/eval_jaxpr/ppermute | solution.py:12
  323.1 9.9 %collective-permute-start.1 = (f32[16,1152]{1,0:T(8,128)S(1)}, f32[16,1152]{1,0:T(8,128)S(1)}, u32[]{:S(2)}, u32[]{:S(2)}) collective-permute-start(f32[16,1152]{1,0:T(8,128)S(1)} %get-tuple-element.411), channel_id=1, source_target_pairs={{0,16},{16,32},{32,48},{48,64},{64,80},{80,96},{96,112},{112,128},... | collective-permute-start | bytes 221192 | tf_op jit(solution)/shard_map/while/body/eval_jaxpr/ppermute | solution.py:12
  335.2 9.9 %collective-permute-start.1 = (f32[16,1152]{1,0:T(8,128)S(1)}, f32[16,1152]{1,0:T(8,128)S(1)}, u32[]{:S(2)}, u32[]{:S(2)}) collective-permute-start(f32[16,1152]{1,0:T(8,128)S(1)} %get-tuple-element.411), channel_id=1, source_target_pairs={{0,16},{16,32},{32,48},{48,64},{64,80},{80,96},{96,112},{112,128},... | collective-permute-start | bytes 221192 | tf_op jit(solution)/shard_map/while/body/eval_jaxpr/ppermute | solution.py:12
  347.2 9.9 %collective-permute-start.1 = (f32[16,1152]{1,0:T(8,128)S(1)}, f32[16,1152]{1,0:T(8,128)S(1)}, u32[]{:S(2)}, u32[]{:S(2)}) collective-permute-start(f32[16,1152]{1,0:T(8,128)S(1)} %get-tuple-element.411), channel_id=1, source_target_pairs={{0,16},{16,32},{32,48},{48,64},{64,80},{80,96},{96,112},{112,128},... | collective-permute-start | bytes 221192 | tf_op jit(solution)/shard_map/while/body/eval_jaxpr/ppermute | solution.py:12
  357.3 9.7 %collective-permute-start = (bf16[16,1152]{1,0:T(8,128)(2,1)S(1)}, bf16[16,1152]{1,0:T(8,128)(2,1)S(1)}, u32[]{:S(2)}, u32[]{:S(2)}) collective-permute-start(bf16[16,1152]{1,0:T(8,128)(2,1)S(1)} %get-tuple-element.410), channel_id=1, source_target_pairs={{0,16},{16,32},{32,48},{48,64},{64,80},{80,96},{96,112},{112,128},... | collective-permute-start | bytes 110600 | tf_op jit(solution)/shard_map/while/body/eval_jaxpr/ppermute | solution.py:12
  359.2 10.1 %collective-permute-start.1 = (f32[16,1152]{1,0:T(8,128)S(1)}, f32[16,1152]{1,0:T(8,128)S(1)}, u32[]{:S(2)}, u32[]{:S(2)}) collective-permute-start(f32[16,1152]{1,0:T(8,128)S(1)} %get-tuple-element.411), channel_id=1, source_target_pairs={{0,16},{16,32},{32,48},{48,64},{64,80},{80,96},{96,112},{112,128},... | collective-permute-start | bytes 221192 | tf_op jit(solution)/shard_map/while/body/eval_jaxpr/ppermute | solution.py:12
  369.6 9.6 %collective-permute-start = (bf16[16,1152]{1,0:T(8,128)(2,1)S(1)}, bf16[16,1152]{1,0:T(8,128)(2,1)S(1)}, u32[]{:S(2)}, u32[]{:S(2)}) collective-permute-start(bf16[16,1152]{1,0:T(8,128)(2,1)S(1)} %get-tuple-element.410), channel_id=1, source_target_pairs={{0,16},{16,32},{32,48},{48,64},{64,80},{80,96},{96,112},{112,128},... | collective-permute-start | bytes 110600 | tf_op jit(solution)/shard_map/while/body/eval_jaxpr/ppermute | solution.py:12
  371.5 10.0 %collective-permute-start.1 = (f32[16,1152]{1,0:T(8,128)S(1)}, f32[16,1152]{1,0:T(8,128)S(1)}, u32[]{:S(2)}, u32[]{:S(2)}) collective-permute-start(f32[16,1152]{1,0:T(8,128)S(1)} %get-tuple-element.411), channel_id=1, source_target_pairs={{0,16},{16,32},{32,48},{48,64},{64,80},{80,96},{96,112},{112,128},... | collective-permute-start | bytes 221192 | tf_op jit(solution)/shard_map/while/body/eval_jaxpr/ppermute | solution.py:12
  383.6 9.9 %collective-permute-start.1 = (f32[16,1152]{1,0:T(8,128)S(1)}, f32[16,1152]{1,0:T(8,128)S(1)}, u32[]{:S(2)}, u32[]{:S(2)}) collective-permute-start(f32[16,1152]{1,0:T(8,128)S(1)} %get-tuple-element.411), channel_id=1, source_target_pairs={{0,16},{16,32},{32,48},{48,64},{64,80},{80,96},{96,112},{112,128},... | collective-permute-start | bytes 221192 | tf_op jit(solution)/shard_map/while/body/eval_jaxpr/ppermute | solution.py:12
  395.6 9.9 %collective-permute-start.1 = (f32[16,1152]{1,0:T(8,128)S(1)}, f32[16,1152]{1,0:T(8,128)S(1)}, u32[]{:S(2)}, u32[]{:S(2)}) collective-permute-start(f32[16,1152]{1,0:T(8,128)S(1)} %get-tuple-element.411), channel_id=1, source_target_pairs={{0,16},{16,32},{32,48},{48,64},{64,80},{80,96},{96,112},{112,128},... | collective-permute-start | bytes 221192 | tf_op jit(solution)/shard_map/while/body/eval_jaxpr/ppermute | solution.py:12
  407.3 10.0 %collective-permute-start.2 = (f32[16,1152]{1,0:T(8,128)S(1)}, f32[16,1152]{1,0:T(8,128)S(1)}, u32[]{:S(2)}, u32[]{:S(2)}) collective-permute-start(f32[16,1152]{1,0:T(8,128)S(1)} %get-tuple-element.271), channel_id=1, source_target_pairs={{0,16},{16,32},{32,48},{48,64},{64,80},{80,96},{96,112},{112,128},... | collective-permute-start | bytes 221192 | tf_op jit(solution)/shard_map/ppermute | solution.py:12
  (34 other events, 373.2 us)
Sparse Core Ops, SparseCore 0:
  407.4 94.3 reduce-scatter.1
where the time goes:
time: 514 us; the launch traced here: 511 us
  starting transfers between devices  234 us (46%)
  waiting for transfers between devices  170 us (33%)
  blocking collectives  42.7 us (8%)
  matrix products  37.2 us (7%)
  between operations  15.4 us (3%)
  other arithmetic  7.44 us (1%)
    ppermute x63, starting transfers between devices, from_behind(): return lax.ppermute(value, axis, pairs)  234 us
    ppermute x63, waiting for transfers between devices, from_behind(): return lax.ppermute(value, axis, pairs)  86.4 us
    reduce_scatter x1, waiting for transfers between devices, per_device(): lax.psum_scatter(image_terms, 'grp', scatter_dimension=0, tiled=True)  83.5 us
    all_gather x1, blocking collectives, per_device(): lax.all_gather(img_unit.astype(jnp.bfloat16), 'grp', axis=0, tiled=True)  42.7 us
    dot_general x32, matrix products, station(): jnp.einsum('id,kd->ik', image_block, moving, preferred_element_type=jnp.f...  29.5 us
  transfers between devices with their start and end apart: 64, of which 37 were waited for; matrix products, arithmetic and copies ran while one was open for 6% of the time, Pallas kernels for 0%

commit v1 on v0

--- a/solution.py
+++ b/solution.py
@@ -41,7 +41,11 @@
     offset = bias[0]
     img_unit, img_length = normalize(image_emb)
     txt_unit, txt_length = normalize(text_emb)
-    image_block = lax.all_gather(img_unit.astype(jnp.bfloat16), "grp", axis=0, tiled=True)
+    x = img_unit.astype(jnp.bfloat16)
+    devices = lax.axis_size("grp")
+    blocks = jnp.stack([x for _ in range(devices)])
+    blocks = lax.all_to_all(blocks, "grp", split_axis=0, concat_axis=0)
+    image_block = jnp.concatenate(blocks, axis=0)
     block_rows = groups * row_count
     image_ids = loop_at * block_rows + jnp.arange(block_rows, dtype=jnp.int32)
     text_rows = txt_unit.astype(jnp.bfloat16)

time: 514 us -> 499 us (0.971)
  the two profiles are of different devices: /device:TPU:4 before, /device:TPU:6 now
where the time goes in v1:
time: 499 us; the launch traced here: 497 us
  starting transfers between devices  325 us (65%)
  waiting for transfers between devices  107 us (21%)
  matrix products  37.3 us (7%)
  between operations  15.5 us (3%)
  other arithmetic  5.92 us (1%)
    ppermute x63, starting transfers between devices, from_behind(): return lax.ppermute(value, axis, pairs)  314 us
    reduce_scatter x1, waiting for transfers between devices, per_device(): lax.psum_scatter(image_terms, 'grp', scatter_dimension=0, tiled=True)  89.8 us
    dot_general x32, matrix products, station(): jnp.einsum('id,kd->ik', image_block, moving, preferred_element_type=jnp.f...  29.5 us
    all_to_all x1, waiting for transfers between devices, per_device(): blocks = lax.all_to_all(blocks, 'grp', split_axis=0, concat_axis=0)  14.9 us
    all_to_all x1, starting transfers between devices, per_device(): blocks = lax.all_to_all(blocks, 'grp', split_axis=0, concat_axis=0)  11.4 us
  transfers between devices with their start and end apart: 65, of which 4 were waited for; matrix products, arithmetic and copies ran while one was open for 6% of the time, Pallas kernels for 0%

profile of v1, /device:TPU:6, one launch (start us, length us, event | category | flops | bytes accessed | tf_op | source)
XLA Modules:
  0.0 496.5 jit_solution(949967155378385466)
XLA Ops:
  9.8 11.4 %all-to-all-start = ((bf16[16,16,1152]{2,1,0:T(8,128)(2,1)}), bf16[16,16,1152]{2,1,0:T(8,128)(2,1)S(1)}, u32[]{:S(2)}, u32[]{:S(2)}) async-start(bf16[16,16,1152]{2,1,0:T(8,128)(2,1)} %stack.2), calls=%async_computation | async-start | bytes 1179648 | tf_op jit(solution)/shard_map/all_to_all | solution.py:47
  23.0 14.9 %all-to-all-done = bf16[16,16,1152]{2,1,0:T(8,128)(2,1)S(1)} async-done(((bf16[16,16,1152]{2,1,0:T(8,128)(2,1)}), bf16[16,16,1152]{2,1,0:T(8,128)(2,1)S(1)}, u32[]{:S(2)}, u32[]{:S(2)}) %all-to-all-start) | async-done | bytes 589856 | tf_op jit(solution)/shard_map/all_to_all | solution.py:47
  38.5 350.6 %while.22 = (s32[]{:T(128)}, bf16[16,1152]{1,0:T(8,128)(2,1)S(1)}, f32[16,1152]{1,0:T(8,128)S(1)}, bf16[256,512]{0,1:T(8,128)(2,1)S(1)}, bf16[512,1152]{1,0:T(8,...) while((s32[]{:T(128)}, bf16[16,1152]{1,0:T(8,128)(2,1)S(1)}, ...), condition=%wide.region_3.4_spmd.clone, body=%wide.region_2.3_spmd.clone.sunk | while | flops 18934052 | bytes 1981456 | solution.py:86
  48.4 7.4 %collective-permute-start.1 = (f32[16,1152]{1,0:T(8,128)S(1)}, f32[16,1152]{1,0:T(8,128)S(1)}, u32[]{:S(2)}, u32[]{:S(2)}) collective-permute-start(f32[16,1152]{1,0:T(8,128)S(1)} %get-tuple-element.411), channel_id=1, source_target_pairs={{0,16},{16,32},{32,48},{48,64},{64,80},{80,96},{96,112},{112,128},... | collective-permute-start | bytes 221192 | tf_op jit(solution)/shard_map/while/body/eval_jaxpr/ppermute | solution.py:12
  59.4 7.3 %collective-permute-start.1 = (f32[16,1152]{1,0:T(8,128)S(1)}, f32[16,1152]{1,0:T(8,128)S(1)}, u32[]{:S(2)}, u32[]{:S(2)}) collective-permute-start(f32[16,1152]{1,0:T(8,128)S(1)} %get-tuple-element.411), channel_id=1, source_target_pairs={{0,16},{16,32},{32,48},{48,64},{64,80},{80,96},{96,112},{112,128},... | collective-permute-start | bytes 221192 | tf_op jit(solution)/shard_map/while/body/eval_jaxpr/ppermute | solution.py:12
  70.2 7.3 %collective-permute-start.1 = (f32[16,1152]{1,0:T(8,128)S(1)}, f32[16,1152]{1,0:T(8,128)S(1)}, u32[]{:S(2)}, u32[]{:S(2)}) collective-permute-start(f32[16,1152]{1,0:T(8,128)S(1)} %get-tuple-element.411), channel_id=1, source_target_pairs={{0,16},{16,32},{32,48},{48,64},{64,80},{80,96},{96,112},{112,128},... | collective-permute-start | bytes 221192 | tf_op jit(solution)/shard_map/while/body/eval_jaxpr/ppermute | solution.py:12
  81.0 7.3 %collective-permute-start.1 = (f32[16,1152]{1,0:T(8,128)S(1)}, f32[16,1152]{1,0:T(8,128)S(1)}, u32[]{:S(2)}, u32[]{:S(2)}) collective-permute-start(f32[16,1152]{1,0:T(8,128)S(1)} %get-tuple-element.411), channel_id=1, source_target_pairs={{0,16},{16,32},{32,48},{48,64},{64,80},{80,96},{96,112},{112,128},... | collective-permute-start | bytes 221192 | tf_op jit(solution)/shard_map/while/body/eval_jaxpr/ppermute | solution.py:12
  91.8 7.3 %collective-permute-start.1 = (f32[16,1152]{1,0:T(8,128)S(1)}, f32[16,1152]{1,0:T(8,128)S(1)}, u32[]{:S(2)}, u32[]{:S(2)}) collective-permute-start(f32[16,1152]{1,0:T(8,128)S(1)} %get-tuple-element.411), channel_id=1, source_target_pairs={{0,16},{16,32},{32,48},{48,64},{64,80},{80,96},{96,112},{112,128},... | collective-permute-start | bytes 221192 | tf_op jit(solution)/shard_map/while/body/eval_jaxpr/ppermute | solution.py:12
  102.7 7.3 %collective-permute-start.1 = (f32[16,1152]{1,0:T(8,128)S(1)}, f32[16,1152]{1,0:T(8,128)S(1)}, u32[]{:S(2)}, u32[]{:S(2)}) collective-permute-start(f32[16,1152]{1,0:T(8,128)S(1)} %get-tuple-element.411), channel_id=1, source_target_pairs={{0,16},{16,32},{32,48},{48,64},{64,80},{80,96},{96,112},{112,128},... | collective-permute-start | bytes 221192 | tf_op jit(solution)/shard_map/while/body/eval_jaxpr/ppermute | solution.py:12
  113.5 7.3 %collective-permute-start.1 = (f32[16,1152]{1,0:T(8,128)S(1)}, f32[16,1152]{1,0:T(8,128)S(1)}, u32[]{:S(2)}, u32[]{:S(2)}) collective-permute-start(f32[16,1152]{1,0:T(8,128)S(1)} %get-tuple-element.411), channel_id=1, source_target_pairs={{0,16},{16,32},{32,48},{48,64},{64,80},{80,96},{96,112},{112,128},... | collective-permute-start | bytes 221192 | tf_op jit(solution)/shard_map/while/body/eval_jaxpr/ppermute | solution.py:12
  124.3 7.3 %collective-permute-start.1 = (f32[16,1152]{1,0:T(8,128)S(1)}, f32[16,1152]{1,0:T(8,128)S(1)}, u32[]{:S(2)}, u32[]{:S(2)}) collective-permute-start(f32[16,1152]{1,0:T(8,128)S(1)} %get-tuple-element.411), channel_id=1, source_target_pairs={{0,16},{16,32},{32,48},{48,64},{64,80},{80,96},{96,112},{112,128},... | collective-permute-start | bytes 221192 | tf_op jit(solution)/shard_map/while/body/eval_jaxpr/ppermute | solution.py:12
  135.8 7.5 %collective-permute-start.1 = (f32[16,1152]{1,0:T(8,128)S(1)}, f32[16,1152]{1,0:T(8,128)S(1)}, u32[]{:S(2)}, u32[]{:S(2)}) collective-permute-start(f32[16,1152]{1,0:T(8,128)S(1)} %get-tuple-element.411), channel_id=1, source_target_pairs={{0,16},{16,32},{32,48},{48,64},{64,80},{80,96},{96,112},{112,128},... | collective-permute-start | bytes 221192 | tf_op jit(solution)/shard_map/while/body/eval_jaxpr/ppermute | solution.py:12
  146.8 7.3 %collective-permute-start.1 = (f32[16,1152]{1,0:T(8,128)S(1)}, f32[16,1152]{1,0:T(8,128)S(1)}, u32[]{:S(2)}, u32[]{:S(2)}) collective-permute-start(f32[16,1152]{1,0:T(8,128)S(1)} %get-tuple-element.411), channel_id=1, source_target_pairs={{0,16},{16,32},{32,48},{48,64},{64,80},{80,96},{96,112},{112,128},... | collective-permute-start | bytes 221192 | tf_op jit(solution)/shard_map/while/body/eval_jaxpr/ppermute | solution.py:12
  158.0 7.4 %collective-permute-start.1 = (f32[16,1152]{1,0:T(8,128)S(1)}, f32[16,1152]{1,0:T(8,128)S(1)}, u32[]{:S(2)}, u32[]{:S(2)}) collective-permute-start(f32[16,1152]{1,0:T(8,128)S(1)} %get-tuple-element.411), channel_id=1, source_target_pairs={{0,16},{16,32},{32,48},{48,64},{64,80},{80,96},{96,112},{112,128},... | collective-permute-start | bytes 221192 | tf_op jit(solution)/shard_map/while/body/eval_jaxpr/ppermute | solution.py:12
  168.9 7.3 %collective-permute-start.1 = (f32[16,1152]{1,0:T(8,128)S(1)}, f32[16,1152]{1,0:T(8,128)S(1)}, u32[]{:S(2)}, u32[]{:S(2)}) collective-permute-start(f32[16,1152]{1,0:T(8,128)S(1)} %get-tuple-element.411), channel_id=1, source_target_pairs={{0,16},{16,32},{32,48},{48,64},{64,80},{80,96},{96,112},{112,128},... | collective-permute-start | bytes 221192 | tf_op jit(solution)/shard_map/while/body/eval_jaxpr/ppermute | solution.py:12
  179.8 7.3 %collective-permute-start.1 = (f32[16,1152]{1,0:T(8,128)S(1)}, f32[16,1152]{1,0:T(8,128)S(1)}, u32[]{:S(2)}, u32[]{:S(2)}) collective-permute-start(f32[16,1152]{1,0:T(8,128)S(1)} %get-tuple-element.411), channel_id=1, source_target_pairs={{0,16},{16,32},{32,48},{48,64},{64,80},{80,96},{96,112},{112,128},... | collective-permute-start | bytes 221192 | tf_op jit(solution)/shard_map/while/body/eval_jaxpr/ppermute | solution.py:12
  190.6 7.3 %collective-permute-start.1 = (f32[16,1152]{1,0:T(8,128)S(1)}, f32[16,1152]{1,0:T(8,128)S(1)}, u32[]{:S(2)}, u32[]{:S(2)}) collective-permute-start(f32[16,1152]{1,0:T(8,128)S(1)} %get-tuple-element.411), channel_id=1, source_target_pairs={{0,16},{16,32},{32,48},{48,64},{64,80},{80,96},{96,112},{112,128},... | collective-permute-start | bytes 221192 | tf_op jit(solution)/shard_map/while/body/eval_jaxpr/ppermute | solution.py:12
  201.4 7.3 %collective-permute-start.1 = (f32[16,1152]{1,0:T(8,128)S(1)}, f32[16,1152]{1,0:T(8,128)S(1)}, u32[]{:S(2)}, u32[]{:S(2)}) collective-permute-start(f32[16,1152]{1,0:T(8,128)S(1)} %get-tuple-element.411), channel_id=1, source_target_pairs={{0,16},{16,32},{32,48},{48,64},{64,80},{80,96},{96,112},{112,128},... | collective-permute-start | bytes 221192 | tf_op jit(solution)/shard_map/while/body/eval_jaxpr/ppermute | solution.py:12
  212.2 7.3 %collective-permute-start.1 = (f32[16,1152]{1,0:T(8,128)S(1)}, f32[16,1152]{1,0:T(8,128)S(1)}, u32[]{:S(2)}, u32[]{:S(2)}) collective-permute-start(f32[16,1152]{1,0:T(8,128)S(1)} %get-tuple-element.411), channel_id=1, source_target_pairs={{0,16},{16,32},{32,48},{48,64},{64,80},{80,96},{96,112},{112,128},... | collective-permute-start | bytes 221192 | tf_op jit(solution)/shard_map/while/body/eval_jaxpr/ppermute | solution.py:12
  224.1 7.3 %collective-permute-start.1 = (f32[16,1152]{1,0:T(8,128)S(1)}, f32[16,1152]{1,0:T(8,128)S(1)}, u32[]{:S(2)}, u32[]{:S(2)}) collective-permute-start(f32[16,1152]{1,0:T(8,128)S(1)} %get-tuple-element.411), channel_id=1, source_target_pairs={{0,16},{16,32},{32,48},{48,64},{64,80},{80,96},{96,112},{112,128},... | collective-permute-start | bytes 221192 | tf_op jit(solution)/shard_map/while/body/eval_jaxpr/ppermute | solution.py:12
  236.1 7.3 %collective-permute-start.1 = (f32[16,1152]{1,0:T(8,128)S(1)}, f32[16,1152]{1,0:T(8,128)S(1)}, u32[]{:S(2)}, u32[]{:S(2)}) collective-permute-start(f32[16,1152]{1,0:T(8,128)S(1)} %get-tuple-element.411), channel_id=1, source_target_pairs={{0,16},{16,32},{32,48},{48,64},{64,80},{80,96},{96,112},{112,128},... | collective-permute-start | bytes 221192 | tf_op jit(solution)/shard_map/while/body/eval_jaxpr/ppermute | solution.py:12
  248.1 7.3 %collective-permute-start.1 = (f32[16,1152]{1,0:T(8,128)S(1)}, f32[16,1152]{1,0:T(8,128)S(1)}, u32[]{:S(2)}, u32[]{:S(2)}) collective-permute-start(f32[16,1152]{1,0:T(8,128)S(1)} %get-tuple-element.411), channel_id=1, source_target_pairs={{0,16},{16,32},{32,48},{48,64},{64,80},{80,96},{96,112},{112,128},... | collective-permute-start | bytes 221192 | tf_op jit(solution)/shard_map/while/body/eval_jaxpr/ppermute | solution.py:12
  260.1 7.3 %collective-permute-start.1 = (f32[16,1152]{1,0:T(8,128)S(1)}, f32[16,1152]{1,0:T(8,128)S(1)}, u32[]{:S(2)}, u32[]{:S(2)}) collective-permute-start(f32[16,1152]{1,0:T(8,128)S(1)} %get-tuple-element.411), channel_id=1, source_target_pairs={{0,16},{16,32},{32,48},{48,64},{64,80},{80,96},{96,112},{112,128},... | collective-permute-start | bytes 221192 | tf_op jit(solution)/shard_map/while/body/eval_jaxpr/ppermute | solution.py:12
  272.2 7.3 %collective-permute-start.1 = (f32[16,1152]{1,0:T(8,128)S(1)}, f32[16,1152]{1,0:T(8,128)S(1)}, u32[]{:S(2)}, u32[]{:S(2)}) collective-permute-start(f32[16,1152]{1,0:T(8,128)S(1)} %get-tuple-element.411), channel_id=1, source_target_pairs={{0,16},{16,32},{32,48},{48,64},{64,80},{80,96},{96,112},{112,128},... | collective-permute-start | bytes 221192 | tf_op jit(solution)/shard_map/while/body/eval_jaxpr/ppermute | solution.py:12
  284.2 7.3 %collective-permute-start.1 = (f32[16,1152]{1,0:T(8,128)S(1)}, f32[16,1152]{1,0:T(8,128)S(1)}, u32[]{:S(2)}, u32[]{:S(2)}) collective-permute-start(f32[16,1152]{1,0:T(8,128)S(1)} %get-tuple-element.411), channel_id=1, source_target_pairs={{0,16},{16,32},{32,48},{48,64},{64,80},{80,96},{96,112},{112,128},... | collective-permute-start | bytes 221192 | tf_op jit(solution)/shard_map/while/body/eval_jaxpr/ppermute | solution.py:12
  296.2 7.3 %collective-permute-start.1 = (f32[16,1152]{1,0:T(8,128)S(1)}, f32[16,1152]{1,0:T(8,128)S(1)}, u32[]{:S(2)}, u32[]{:S(2)}) collective-permute-start(f32[16,1152]{1,0:T(8,128)S(1)} %get-tuple-element.411), channel_id=1, source_target_pairs={{0,16},{16,32},{32,48},{48,64},{64,80},{80,96},{96,112},{112,128},... | collective-permute-start | bytes 221192 | tf_op jit(solution)/shard_map/while/body/eval_jaxpr/ppermute | solution.py:12
  308.3 7.3 %collective-permute-start.1 = (f32[16,1152]{1,0:T(8,128)S(1)}, f32[16,1152]{1,0:T(8,128)S(1)}, u32[]{:S(2)}, u32[]{:S(2)}) collective-permute-start(f32[16,1152]{1,0:T(8,128)S(1)} %get-tuple-element.411), channel_id=1, source_target_pairs={{0,16},{16,32},{32,48},{48,64},{64,80},{80,96},{96,112},{112,128},... | collective-permute-start | bytes 221192 | tf_op jit(solution)/shard_map/while/body/eval_jaxpr/ppermute | solution.py:12
  320.3 7.3 %collective-permute-start.1 = (f32[16,1152]{1,0:T(8,128)S(1)}, f32[16,1152]{1,0:T(8,128)S(1)}, u32[]{:S(2)}, u32[]{:S(2)}) collective-permute-start(f32[16,1152]{1,0:T(8,128)S(1)} %get-tuple-element.411), channel_id=1, source_target_pairs={{0,16},{16,32},{32,48},{48,64},{64,80},{80,96},{96,112},{112,128},... | collective-permute-start | bytes 221192 | tf_op jit(solution)/shard_map/while/body/eval_jaxpr/ppermute | solution.py:12
  332.3 7.3 %collective-permute-start.1 = (f32[16,1152]{1,0:T(8,128)S(1)}, f32[16,1152]{1,0:T(8,128)S(1)}, u32[]{:S(2)}, u32[]{:S(2)}) collective-permute-start(f32[16,1152]{1,0:T(8,128)S(1)} %get-tuple-element.411), channel_id=1, source_target_pairs={{0,16},{16,32},{32,48},{48,64},{64,80},{80,96},{96,112},{112,128},... | collective-permute-start | bytes 221192 | tf_op jit(solution)/shard_map/while/body/eval_jaxpr/ppermute | solution.py:12
  356.4 7.3 %collective-permute-start.1 = (f32[16,1152]{1,0:T(8,128)S(1)}, f32[16,1152]{1,0:T(8,128)S(1)}, u32[]{:S(2)}, u32[]{:S(2)}) collective-permute-start(f32[16,1152]{1,0:T(8,128)S(1)} %get-tuple-element.411), channel_id=1, source_target_pairs={{0,16},{16,32},{32,48},{48,64},{64,80},{80,96},{96,112},{112,128},... | collective-permute-start | bytes 221192 | tf_op jit(solution)/shard_map/while/body/eval_jaxpr/ppermute | solution.py:12
  368.4 7.3 %collective-permute-start.1 = (f32[16,1152]{1,0:T(8,128)S(1)}, f32[16,1152]{1,0:T(8,128)S(1)}, u32[]{:S(2)}, u32[]{:S(2)}) collective-permute-start(f32[16,1152]{1,0:T(8,128)S(1)} %get-tuple-element.411), channel_id=1, source_target_pairs={{0,16},{16,32},{32,48},{48,64},{64,80},{80,96},{96,112},{112,128},... | collective-permute-start | bytes 221192 | tf_op jit(solution)/shard_map/while/body/eval_jaxpr/ppermute | solution.py:12
  397.2 89.8 %reduce-scatter.2.cloned.1.call-done = f32[16,1152]{1,0:T(8,128)} async-done(((f32[256,1152]{1,0:T(8,128)}), f32[16,1152]{1,0:T(8,128)}) %reduce-scatter.2.cloned.1.call-update) | async-done | bytes 73744 | tf_op jit(solution)/shard_map/reduce_scatter | solution.py:91
  (308 shorter events, 156.7 us)
Async XLA Ops:
  9.8 28.1 %all-to-all-start = ((bf16[16,16,1152]{2,1,0:T(8,128)(2,1)}), bf16[16,16,1152]{2,1,0:T(8,128)(2,1)S(1)}, u32[]{:S(2)}, u32[]{:S(2)}) async-start(bf16[16,16,1152]{2,1,0:T(8,128)(2,1)} %stack.2), calls=%async_computation | async-start | bytes 1179648 | tf_op jit(solution)/shard_map/all_to_all | solution.py:47
  21.2 465.8 %reduce-scatter.2.cloned.1.call-start = ((), (), s32[]{:S(2)}) async-start(), calls=%async_computation.2 | async-start | bytes 1253376 | tf_op jit(solution)/shard_map/reduce_scatter | solution.py:91
  46.3 9.6 %collective-permute-start = (bf16[16,1152]{1,0:T(8,128)(2,1)S(1)}, bf16[16,1152]{1,0:T(8,128)(2,1)S(1)}, u32[]{:S(2)}, u32[]{:S(2)}) collective-permute-start(bf16[16,1152]{1,0:T(8,128)(2,1)S(1)} %get-tuple-element.410), channel_id=1, source_target_pairs={{0,16},{16,32},{32,48},{48,64},{64,80},{80,96},{96,112},{112,128},... | collective-permute-start | bytes 110600 | tf_op jit(solution)/shard_map/while/body/eval_jaxpr/ppermute | solution.py:12
  57.1 9.6 %collective-permute-start = (bf16[16,1152]{1,0:T(8,128)(2,1)S(1)}, bf16[16,1152]{1,0:T(8,128)(2,1)S(1)}, u32[]{:S(2)}, u32[]{:S(2)}) collective-permute-start(bf16[16,1152]{1,0:T(8,128)(2,1)S(1)} %get-tuple-element.410), channel_id=1, source_target_pairs={{0,16},{16,32},{32,48},{48,64},{64,80},{80,96},{96,112},{112,128},... | collective-permute-start | bytes 110600 | tf_op jit(solution)/shard_map/while/body/eval_jaxpr/ppermute | solution.py:12
  67.9 9.6 %collective-permute-start = (bf16[16,1152]{1,0:T(8,128)(2,1)S(1)}, bf16[16,1152]{1,0:T(8,128)(2,1)S(1)}, u32[]{:S(2)}, u32[]{:S(2)}) collective-permute-start(bf16[16,1152]{1,0:T(8,128)(2,1)S(1)} %get-tuple-element.410), channel_id=1, source_target_pairs={{0,16},{16,32},{32,48},{48,64},{64,80},{80,96},{96,112},{112,128},... | collective-permute-start | bytes 110600 | tf_op jit(solution)/shard_map/while/body/eval_jaxpr/ppermute | solution.py:12
  78.8 9.6 %collective-permute-start = (bf16[16,1152]{1,0:T(8,128)(2,1)S(1)}, bf16[16,1152]{1,0:T(8,128)(2,1)S(1)}, u32[]{:S(2)}, u32[]{:S(2)}) collective-permute-start(bf16[16,1152]{1,0:T(8,128)(2,1)S(1)} %get-tuple-element.410), channel_id=1, source_target_pairs={{0,16},{16,32},{32,48},{48,64},{64,80},{80,96},{96,112},{112,128},... | collective-permute-start | bytes 110600 | tf_op jit(solution)/shard_map/while/body/eval_jaxpr/ppermute | solution.py:12
  89.6 9.6 %collective-permute-start = (bf16[16,1152]{1,0:T(8,128)(2,1)S(1)}, bf16[16,1152]{1,0:T(8,128)(2,1)S(1)}, u32[]{:S(2)}, u32[]{:S(2)}) collective-permute-start(bf16[16,1152]{1,0:T(8,128)(2,1)S(1)} %get-tuple-element.410), channel_id=1, source_target_pairs={{0,16},{16,32},{32,48},{48,64},{64,80},{80,96},{96,112},{112,128},... | collective-permute-start | bytes 110600 | tf_op jit(solution)/shard_map/while/body/eval_jaxpr/ppermute | solution.py:12
  100.4 9.6 %collective-permute-start = (bf16[16,1152]{1,0:T(8,128)(2,1)S(1)}, bf16[16,1152]{1,0:T(8,128)(2,1)S(1)}, u32[]{:S(2)}, u32[]{:S(2)}) collective-permute-start(bf16[16,1152]{1,0:T(8,128)(2,1)S(1)} %get-tuple-element.410), channel_id=1, source_target_pairs={{0,16},{16,32},{32,48},{48,64},{64,80},{80,96},{96,112},{112,128},... | collective-permute-start | bytes 110600 | tf_op jit(solution)/shard_map/while/body/eval_jaxpr/ppermute | solution.py:12
  111.2 9.6 %collective-permute-start = (bf16[16,1152]{1,0:T(8,128)(2,1)S(1)}, bf16[16,1152]{1,0:T(8,128)(2,1)S(1)}, u32[]{:S(2)}, u32[]{:S(2)}) collective-permute-start(bf16[16,1152]{1,0:T(8,128)(2,1)S(1)} %get-tuple-element.410), channel_id=1, source_target_pairs={{0,16},{16,32},{32,48},{48,64},{64,80},{80,96},{96,112},{112,128},... | collective-permute-start | bytes 110600 | tf_op jit(solution)/shard_map/while/body/eval_jaxpr/ppermute | solution.py:12
  122.0 9.6 %collective-permute-start = (bf16[16,1152]{1,0:T(8,128)(2,1)S(1)}, bf16[16,1152]{1,0:T(8,128)(2,1)S(1)}, u32[]{:S(2)}, u32[]{:S(2)}) collective-permute-start(bf16[16,1152]{1,0:T(8,128)(2,1)S(1)} %get-tuple-element.410), channel_id=1, source_target_pairs={{0,16},{16,32},{32,48},{48,64},{64,80},{80,96},{96,112},{112,128},... | collective-permute-start | bytes 110600 | tf_op jit(solution)/shard_map/while/body/eval_jaxpr/ppermute | solution.py:12
  132.9 10.5 %collective-permute-start = (bf16[16,1152]{1,0:T(8,128)(2,1)S(1)}, bf16[16,1152]{1,0:T(8,128)(2,1)S(1)}, u32[]{:S(2)}, u32[]{:S(2)}) collective-permute-start(bf16[16,1152]{1,0:T(8,128)(2,1)S(1)} %get-tuple-element.410), channel_id=1, source_target_pairs={{0,16},{16,32},{32,48},{48,64},{64,80},{80,96},{96,112},{112,128},... | collective-permute-start | bytes 110600 | tf_op jit(solution)/shard_map/while/body/eval_jaxpr/ppermute | solution.py:12
  144.6 9.7 %collective-permute-start = (bf16[16,1152]{1,0:T(8,128)(2,1)S(1)}, bf16[16,1152]{1,0:T(8,128)(2,1)S(1)}, u32[]{:S(2)}, u32[]{:S(2)}) collective-permute-start(bf16[16,1152]{1,0:T(8,128)(2,1)S(1)} %get-tuple-element.410), channel_id=1, source_target_pairs={{0,16},{16,32},{32,48},{48,64},{64,80},{80,96},{96,112},{112,128},... | collective-permute-start | bytes 110600 | tf_op jit(solution)/shard_map/while/body/eval_jaxpr/ppermute | solution.py:12
  155.4 10.0 %collective-permute-start = (bf16[16,1152]{1,0:T(8,128)(2,1)S(1)}, bf16[16,1152]{1,0:T(8,128)(2,1)S(1)}, u32[]{:S(2)}, u32[]{:S(2)}) collective-permute-start(bf16[16,1152]{1,0:T(8,128)(2,1)S(1)} %get-tuple-element.410), channel_id=1, source_target_pairs={{0,16},{16,32},{32,48},{48,64},{64,80},{80,96},{96,112},{112,128},... | collective-permute-start | bytes 110600 | tf_op jit(solution)/shard_map/while/body/eval_jaxpr/ppermute | solution.py:12
  166.7 9.6 %collective-permute-start = (bf16[16,1152]{1,0:T(8,128)(2,1)S(1)}, bf16[16,1152]{1,0:T(8,128)(2,1)S(1)}, u32[]{:S(2)}, u32[]{:S(2)}) collective-permute-start(bf16[16,1152]{1,0:T(8,128)(2,1)S(1)} %get-tuple-element.410), channel_id=1, source_target_pairs={{0,16},{16,32},{32,48},{48,64},{64,80},{80,96},{96,112},{112,128},... | collective-permute-start | bytes 110600 | tf_op jit(solution)/shard_map/while/body/eval_jaxpr/ppermute | solution.py:12
  177.5 9.6 %collective-permute-start = (bf16[16,1152]{1,0:T(8,128)(2,1)S(1)}, bf16[16,1152]{1,0:T(8,128)(2,1)S(1)}, u32[]{:S(2)}, u32[]{:S(2)}) collective-permute-start(bf16[16,1152]{1,0:T(8,128)(2,1)S(1)} %get-tuple-element.410), channel_id=1, source_target_pairs={{0,16},{16,32},{32,48},{48,64},{64,80},{80,96},{96,112},{112,128},... | collective-permute-start | bytes 110600 | tf_op jit(solution)/shard_map/while/body/eval_jaxpr/ppermute | solution.py:12
  188.3 9.6 %collective-permute-start = (bf16[16,1152]{1,0:T(8,128)(2,1)S(1)}, bf16[16,1152]{1,0:T(8,128)(2,1)S(1)}, u32[]{:S(2)}, u32[]{:S(2)}) collective-permute-start(bf16[16,1152]{1,0:T(8,128)(2,1)S(1)} %get-tuple-element.410), channel_id=1, source_target_pairs={{0,16},{16,32},{32,48},{48,64},{64,80},{80,96},{96,112},{112,128},... | collective-permute-start | bytes 110600 | tf_op jit(solution)/shard_map/while/body/eval_jaxpr/ppermute | solution.py:12
  199.2 9.6 %collective-permute-start = (bf16[16,1152]{1,0:T(8,128)(2,1)S(1)}, bf16[16,1152]{1,0:T(8,128)(2,1)S(1)}, u32[]{:S(2)}, u32[]{:S(2)}) collective-permute-start(bf16[16,1152]{1,0:T(8,128)(2,1)S(1)} %get-tuple-element.410), channel_id=1, source_target_pairs={{0,16},{16,32},{32,48},{48,64},{64,80},{80,96},{96,112},{112,128},... | collective-permute-start | bytes 110600 | tf_op jit(solution)/shard_map/while/body/eval_jaxpr/ppermute | solution.py:12
  210.0 9.6 %collective-permute-start = (bf16[16,1152]{1,0:T(8,128)(2,1)S(1)}, bf16[16,1152]{1,0:T(8,128)(2,1)S(1)}, u32[]{:S(2)}, u32[]{:S(2)}) collective-permute-start(bf16[16,1152]{1,0:T(8,128)(2,1)S(1)} %get-tuple-element.410), channel_id=1, source_target_pairs={{0,16},{16,32},{32,48},{48,64},{64,80},{80,96},{96,112},{112,128},... | collective-permute-start | bytes 110600 | tf_op jit(solution)/shard_map/while/body/eval_jaxpr/ppermute | solution.py:12
  220.8 10.6 %collective-permute-start = (bf16[16,1152]{1,0:T(8,128)(2,1)S(1)}, bf16[16,1152]{1,0:T(8,128)(2,1)S(1)}, u32[]{:S(2)}, u32[]{:S(2)}) collective-permute-start(bf16[16,1152]{1,0:T(8,128)(2,1)S(1)} %get-tuple-element.410), channel_id=1, source_target_pairs={{0,16},{16,32},{32,48},{48,64},{64,80},{80,96},{96,112},{112,128},... | collective-permute-start | bytes 110600 | tf_op jit(solution)/shard_map/while/body/eval_jaxpr/ppermute | solution.py:12
  232.6 10.8 %collective-permute-start = (bf16[16,1152]{1,0:T(8,128)(2,1)S(1)}, bf16[16,1152]{1,0:T(8,128)(2,1)S(1)}, u32[]{:S(2)}, u32[]{:S(2)}) collective-permute-start(bf16[16,1152]{1,0:T(8,128)(2,1)S(1)} %get-tuple-element.410), channel_id=1, source_target_pairs={{0,16},{16,32},{32,48},{48,64},{64,80},{80,96},{96,112},{112,128},... | collective-permute-start | bytes 110600 | tf_op jit(solution)/shard_map/while/body/eval_jaxpr/ppermute | solution.py:12
  244.7 10.8 %collective-permute-start = (bf16[16,1152]{1,0:T(8,128)(2,1)S(1)}, bf16[16,1152]{1,0:T(8,128)(2,1)S(1)}, u32[]{:S(2)}, u32[]{:S(2)}) collective-permute-start(bf16[16,1152]{1,0:T(8,128)(2,1)S(1)} %get-tuple-element.410), channel_id=1, source_target_pairs={{0,16},{16,32},{32,48},{48,64},{64,80},{80,96},{96,112},{112,128},... | collective-permute-start | bytes 110600 | tf_op jit(solution)/shard_map/while/body/eval_jaxpr/ppermute | solution.py:12
  256.7 10.8 %collective-permute-start = (bf16[16,1152]{1,0:T(8,128)(2,1)S(1)}, bf16[16,1152]{1,0:T(8,128)(2,1)S(1)}, u32[]{:S(2)}, u32[]{:S(2)}) collective-permute-start(bf16[16,1152]{1,0:T(8,128)(2,1)S(1)} %get-tuple-element.410), channel_id=1, source_target_pairs={{0,16},{16,32},{32,48},{48,64},{64,80},{80,96},{96,112},{112,128},... | collective-permute-start | bytes 110600 | tf_op jit(solution)/shard_map/while/body/eval_jaxpr/ppermute | solution.py:12
  268.7 10.8 %collective-permute-start = (bf16[16,1152]{1,0:T(8,128)(2,1)S(1)}, bf16[16,1152]{1,0:T(8,128)(2,1)S(1)}, u32[]{:S(2)}, u32[]{:S(2)}) collective-permute-start(bf16[16,1152]{1,0:T(8,128)(2,1)S(1)} %get-tuple-element.410), channel_id=1, source_target_pairs={{0,16},{16,32},{32,48},{48,64},{64,80},{80,96},{96,112},{112,128},... | collective-permute-start | bytes 110600 | tf_op jit(solution)/shard_map/while/body/eval_jaxpr/ppermute | solution.py:12
  280.7 10.8 %collective-permute-start = (bf16[16,1152]{1,0:T(8,128)(2,1)S(1)}, bf16[16,1152]{1,0:T(8,128)(2,1)S(1)}, u32[]{:S(2)}, u32[]{:S(2)}) collective-permute-start(bf16[16,1152]{1,0:T(8,128)(2,1)S(1)} %get-tuple-element.410), channel_id=1, source_target_pairs={{0,16},{16,32},{32,48},{48,64},{64,80},{80,96},{96,112},{112,128},... | collective-permute-start | bytes 110600 | tf_op jit(solution)/shard_map/while/body/eval_jaxpr/ppermute | solution.py:12
  292.8 10.8 %collective-permute-start = (bf16[16,1152]{1,0:T(8,128)(2,1)S(1)}, bf16[16,1152]{1,0:T(8,128)(2,1)S(1)}, u32[]{:S(2)}, u32[]{:S(2)}) collective-permute-start(bf16[16,1152]{1,0:T(8,128)(2,1)S(1)} %get-tuple-element.410), channel_id=1, source_target_pairs={{0,16},{16,32},{32,48},{48,64},{64,80},{80,96},{96,112},{112,128},... | collective-permute-start | bytes 110600 | tf_op jit(solution)/shard_map/while/body/eval_jaxpr/ppermute | solution.py:12
  304.8 10.8 %collective-permute-start = (bf16[16,1152]{1,0:T(8,128)(2,1)S(1)}, bf16[16,1152]{1,0:T(8,128)(2,1)S(1)}, u32[]{:S(2)}, u32[]{:S(2)}) collective-permute-start(bf16[16,1152]{1,0:T(8,128)(2,1)S(1)} %get-tuple-element.410), channel_id=1, source_target_pairs={{0,16},{16,32},{32,48},{48,64},{64,80},{80,96},{96,112},{112,128},... | collective-permute-start | bytes 110600 | tf_op jit(solution)/shard_map/while/body/eval_jaxpr/ppermute | solution.py:12
  316.8 10.8 %collective-permute-start = (bf16[16,1152]{1,0:T(8,128)(2,1)S(1)}, bf16[16,1152]{1,0:T(8,128)(2,1)S(1)}, u32[]{:S(2)}, u32[]{:S(2)}) collective-permute-start(bf16[16,1152]{1,0:T(8,128)(2,1)S(1)} %get-tuple-element.410), channel_id=1, source_target_pairs={{0,16},{16,32},{32,48},{48,64},{64,80},{80,96},{96,112},{112,128},... | collective-permute-start | bytes 110600 | tf_op jit(solution)/shard_map/while/body/eval_jaxpr/ppermute | solution.py:12
  328.9 10.8 %collective-permute-start = (bf16[16,1152]{1,0:T(8,128)(2,1)S(1)}, bf16[16,1152]{1,0:T(8,128)(2,1)S(1)}, u32[]{:S(2)}, u32[]{:S(2)}) collective-permute-start(bf16[16,1152]{1,0:T(8,128)(2,1)S(1)} %get-tuple-element.410), channel_id=1, source_target_pairs={{0,16},{16,32},{32,48},{48,64},{64,80},{80,96},{96,112},{112,128},... | collective-permute-start | bytes 110600 | tf_op jit(solution)/shard_map/while/body/eval_jaxpr/ppermute | solution.py:12
  340.9 10.8 %collective-permute-start = (bf16[16,1152]{1,0:T(8,128)(2,1)S(1)}, bf16[16,1152]{1,0:T(8,128)(2,1)S(1)}, u32[]{:S(2)}, u32[]{:S(2)}) collective-permute-start(bf16[16,1152]{1,0:T(8,128)(2,1)S(1)} %get-tuple-element.410), channel_id=1, source_target_pairs={{0,16},{16,32},{32,48},{48,64},{64,80},{80,96},{96,112},{112,128},... | collective-permute-start | bytes 110600 | tf_op jit(solution)/shard_map/while/body/eval_jaxpr/ppermute | solution.py:12
  352.9 10.8 %collective-permute-start = (bf16[16,1152]{1,0:T(8,128)(2,1)S(1)}, bf16[16,1152]{1,0:T(8,128)(2,1)S(1)}, u32[]{:S(2)}, u32[]{:S(2)}) collective-permute-start(bf16[16,1152]{1,0:T(8,128)(2,1)S(1)} %get-tuple-element.410), channel_id=1, source_target_pairs={{0,16},{16,32},{32,48},{48,64},{64,80},{80,96},{96,112},{112,128},... | collective-permute-start | bytes 110600 | tf_op jit(solution)/shard_map/while/body/eval_jaxpr/ppermute | solution.py:12
  365.0 10.8 %collective-permute-start = (bf16[16,1152]{1,0:T(8,128)(2,1)S(1)}, bf16[16,1152]{1,0:T(8,128)(2,1)S(1)}, u32[]{:S(2)}, u32[]{:S(2)}) collective-permute-start(bf16[16,1152]{1,0:T(8,128)(2,1)S(1)} %get-tuple-element.410), channel_id=1, source_target_pairs={{0,16},{16,32},{32,48},{48,64},{64,80},{80,96},{96,112},{112,128},... | collective-permute-start | bytes 110600 | tf_op jit(solution)/shard_map/while/body/eval_jaxpr/ppermute | solution.py:12
  377.0 10.8 %collective-permute-start = (bf16[16,1152]{1,0:T(8,128)(2,1)S(1)}, bf16[16,1152]{1,0:T(8,128)(2,1)S(1)}, u32[]{:S(2)}, u32[]{:S(2)}) collective-permute-start(bf16[16,1152]{1,0:T(8,128)(2,1)S(1)} %get-tuple-element.410), channel_id=1, source_target_pairs={{0,16},{16,32},{32,48},{48,64},{64,80},{80,96},{96,112},{112,128},... | collective-permute-start | bytes 110600 | tf_op jit(solution)/shard_map/while/body/eval_jaxpr/ppermute | solution.py:12
  (35 other events, 380.8 us)
Sparse Core Ops, SparseCore 0:
  390.7 96.2 reduce-scatter.1
